TPU v7x, 256 devices: a whole 4x4x8 slice. The times are simulated.
256 devices in a mesh: mp: 2 (over y_lo), vocab: 64 (over x, z, core), rows: 2 (over y_hi).
Axes of the slice: x: 4, y: 4 (y_hi: 2, y_lo: 2; y = y_hi * 2 + y_lo), z: 8, core: 2. Of those that a mesh axis runs over, the one named last changes fastest.
Arguments:
- hidden: bfloat16 [2, 512, 4096], P('mp', None, 'rows')
- norm_gain: bfloat16 [2, 4096], P('mp', 'rows'), may hold values from 0.5 to 1.5
- head_weights: bfloat16 [2, 4096, 98304], P('mp', 'rows', 'vocab')
- pair_source: int32 [256], P('vocab'), may hold values from 0 to 191, as said below
- pair_target: int32 [256], P('vocab'), may hold values from 0 to 191, as said below
- pair_count: int32 [64], P('vocab'), may hold values from 2 to 4, as said below
- pair_weight: bfloat16 [256, 512, 512], P('vocab'), may hold values from 0.00019454956 to 0.00390625
- next_token: int32 [512], P(('mp', 'rows')), may hold values from 0 to 98303
Outputs:
- ensemble_logp: float32 [512, 98304], P(('mp', 'rows'), 'vocab')
- target_nll: float32 [512], P(('mp', 'rows'))
Inputs may be any that keep to these rules, and one draw needn't show every extreme that they name: `pair_target`: slot p targets one of the blocks of its own shard, (p // 4) * 3 to (p // 4) * 3 + 2. `pair_source`: slot p's source block lies from (p // 4) * 3 - 3 to (p // 4) * 3 + 2 * 3 - 1; slot 0 of every shard but the first and the last takes the block just below the shard's own, slot 1 of every shard but the last the block just above. The live slots of a shard are its first pair_count ones.
All inputs are finite; a program needn't handle non-finite values.
Results may differ from a plain program's by a relative error of at most 0.0003.
Values may be sent and summed in bfloat16 or wider, within the bound.
A program may use at most 128 MiB of HBM per device.

v0:
```python
import jax
import jax.numpy as jnp
from jax import lax
from jax.sharding import PartitionSpec as P


def with_halo(block, sides, width):
    for axis, dim in sides:
        count = lax.axis_size(axis)
        forward = [(i, i + 1) for i in range(count - 1)]
        backward = [(target, source) for source, target in forward]
        low = lax.ppermute(
            lax.slice_in_dim(block, block.shape[dim] - width, None, axis=dim), axis, forward
        )
        high = lax.ppermute(lax.slice_in_dim(block, 0, width, axis=dim), axis, backward)
        block = jnp.concatenate([low, block, high], axis=dim)
    return block


def on_device(
    hidden, norm_gain, head_weights, pair_source, pair_target, pair_count, pair_weight, next_token
):
    model_count = lax.axis_size("mp")
    row_groups = lax.axis_size("rows")
    rows_all = hidden.shape[1]
    feat_local = hidden.shape[2]
    features = feat_local * row_groups
    half_rows = rows_all // row_groups
    quarter = half_rows // model_count
    head_local = head_weights[0]
    shard_cols = head_local.shape[1]
    block_cols = pair_weight.shape[1]
    blocks_dev = shard_cols // block_cols
    reordered = hidden[0].reshape(model_count, row_groups, quarter, feat_local)
    reordered = jnp.transpose(reordered, (1, 0, 2, 3)).reshape(rows_all, feat_local)
    own_rows = reordered.astype(jnp.float32)
    squares = lax.psum(jnp.sum(own_rows * own_rows, axis=1), "rows")
    row_scale = lax.rsqrt(squares / features + 1e-05)
    normed = own_rows * row_scale[:, None] * norm_gain[0].astype(jnp.float32)[None, :]
    head_wide = head_local.astype(jnp.float32)
    logits = lax.psum_scatter(
        jnp.dot(
            normed, head_wide, preferred_element_type=jnp.float32, precision=lax.Precision.HIGHEST
        ),
        "rows",
        scatter_dimension=0,
        tiled=True,
    )
    row_peak = lax.pmax(jnp.max(logits, axis=1), "vocab")
    row_total = lax.psum(jnp.sum(jnp.exp(logits - row_peak[:, None]), axis=1), "vocab")
    grouped = logits.reshape(model_count, quarter, shard_cols)
    peak_group = row_peak.reshape(model_count, quarter)
    total_group = row_total.reshape(model_count, quarter)
    padded = with_halo(grouped, (("vocab", 2),), shard_cols)
    received, peak_pair, total_pair = (
        lax.all_to_all(padded, "mp", split_axis=0, concat_axis=0, tiled=True),
        lax.all_to_all(peak_group, "mp", split_axis=0, concat_axis=0, tiled=True),
        lax.all_to_all(total_group, "mp", split_axis=0, concat_axis=0, tiled=True),
    )
    llama_part = received[0][:, shard_cols : 2 * shard_cols]
    qwen_part = received[1]
    llama_logp = llama_part - peak_pair[0][:, None] - jnp.log(total_pair[0])[:, None]
    qwen_prob = (jnp.exp(qwen_part - peak_pair[1][:, None]) / total_pair[1][:, None]).astype(
        jnp.bfloat16
    )
    vocab_index = lax.axis_index("vocab")
    source_local = pair_source - (vocab_index * blocks_dev - blocks_dev)
    target_local = pair_target - vocab_index * blocks_dev
    blocks = qwen_prob.reshape(quarter, 3 * blocks_dev, block_cols)
    picked_blocks = jnp.take(blocks, source_local, axis=1)
    contribution = jnp.einsum(
        "qsk,skn->sqn", picked_blocks, pair_weight, preferred_element_type=jnp.float32
    )
    live_slot = jnp.arange(pair_source.shape[0]) < pair_count[0]
    selector = (
        (target_local[:, None] == jnp.arange(blocks_dev)[None, :]) & live_slot[:, None]
    ).astype(jnp.float32)
    mapped = jnp.einsum(
        "sqn,sb->qbn", contribution, selector, precision=lax.Precision.HIGHEST
    ).reshape(quarter, shard_cols)
    mixed = jnp.logaddexp(jnp.maximum(llama_logp, -50.0), jnp.log(mapped))
    columns = vocab_index * shard_cols + jnp.arange(shard_cols, dtype=jnp.int32)
    on_target = next_token[:, None] == columns[None, :]
    picked = jnp.sum(jnp.where(on_target, mixed, 0.0), axis=1)
    row_mass, picked = lax.psum((jnp.sum(mapped, axis=1), picked), "vocab")
    log_norm = jnp.log1p(row_mass)
    return (mixed - log_norm[:, None], log_norm - picked)


def solution(mesh):
    in_specs = (
        P("mp", None, "rows"),
        P("mp", "rows"),
        P("mp", "rows", "vocab"),
        P("vocab"),
        P("vocab"),
        P("vocab"),
        P("vocab", None, None),
        P(("mp", "rows")),
    )
    out_specs = (P(("mp", "rows"), "vocab"), P(("mp", "rows")))
    return jax.shard_map(
        on_device, mesh=mesh, in_specs=in_specs, out_specs=out_specs, check_vma=False
    )
```

profile of v0, /device:TPU:1, one launch (start us, length us, event | category | flops | bytes accessed | tf_op | source)
XLA Modules:
  0.0 584.3 jit_solution(1352087490072054529)
XLA Ops:
  7.2 2.2 fusion.4
  9.4 6.1 %psum.28 = f32[512]{0:T(512)S(1)} all-reduce(f32[512]{0:T(512)S(1)} %bitcast.69), channel_id=1, replica_groups=mesh['mp'=2,'vocab'=64,'rows'=2] {'rows'}, use_global_device_ids=true, to_apply=%region_1.0 | all-reduce | flops 512 | bytes 4096 | tf_op jit(solution)/shard_map/psum | solution.py:37
  16.2 2.2 fusion.5
  20.2 11.6 %fusion = f32[512,1536]{1,0:T(8,128)} fusion(f32[512,2048]{1,0:T(8,128)S(1)} %bitcast.67, bf16[1,2048,1536]{2,1,0:T(8,128)(2,1)S(1)} %bitcast.73), kind=kOutput, calls=%fused_computation.1 | convolution fusion | flops 19327352832 | bytes 13631488 | tf_op jit(solution)/shard_map/dot_general | solution.py:42
  31.8 54.3 %reduce-scatter.2.cloned.1.call-done = f32[256,1536]{1,0:T(8,128)} async-done(((f32[512,1536]{1,0:T(8,128)}), f32[256,1536]{1,0:T(8,128)}) %reduce-scatter.2.cloned.1.call-update) | async-done | bytes 1572880 | tf_op jit(solution)/shard_map/reduce_scatter | solution.py:41
  86.1 3.1 copy.37
  89.2 2.6 collective-permute-start.1
  91.7 3.1 collective-permute-start
  96.4 134.3 %pmax.7 = f32[256]{0:T(256)} all-reduce(f32[256]{0:T(256)S(1)} %reduce_max.9), channel_id=1, replica_groups=mesh['mp'=2,'vocab'=64,'rows'=2] {'vocab'}, use_global_device_ids=true, to_apply=%region_4.0 | all-reduce | flops 256 | bytes 2048 | tf_op jit(solution)/shard_map/pmax | solution.py:49
  230.7 1.8 exponential_reduce_fusion
  232.5 123.6 %psum.29 = f32[2,1,128]{2,1,0:T(1,128)S(1)} all-reduce(f32[2,1,128]{2,1,0:T(1,128)S(1)} %bitcast.71), channel_id=1, replica_groups=mesh['mp'=2,'vocab'=64,'rows'=2] {'vocab'}, use_global_device_ids=true, to_apply=%region_6.0 | all-reduce | flops 256 | bytes 2048 | tf_op jit(solution)/shard_map/psum | solution.py:50
  356.1 4.9 all_to_all.23
  361.0 3.2 all-to-all-start.1
  364.2 4.8 pad_maximum_fusion
  369.0 6.1 %all-to-all-start = ((f32[2,128,4608]{1,2,0:T(8,128)}), f32[2,128,4608]{1,2,0:T(8,128)}, u32[]{:S(2)}, u32[]{:S(2)}) async-start(f32[2,128,4608]{1,2,0:T(8,128)} %pad_maximum_fusion), calls=%async_computation.1 | async-start | bytes 9437184 | tf_op jit(solution)/shard_map/all_to_all | solution.py:56
  375.9 50.1 %all-to-all-done = f32[2,128,4608]{1,2,0:T(8,128)} async-done(((f32[2,128,4608]{1,2,0:T(8,128)}), f32[2,128,4608]{1,2,0:T(8,128)}, u32[]{:S(2)}, u32[]{:S(2)}) %all-to-all-start) | async-done | bytes 4718624 | tf_op jit(solution)/shard_map/all_to_all | solution.py:56
  426.0 4.8 slice_bitcast_fusion
  430.8 3.2 copy.40
  434.0 2.1 divide_convert_fusion
  439.0 3.1 log_bitcast_fusion
  443.7 1.9 select_reduce_fusion
  445.5 126.5 %all-reduce = (f32[128]{0:T(128)S(1)}, f32[128]{0:T(128)S(1)}) all-reduce(f32[128]{0:T(128)S(1)} %get-tuple-element.17, f32[128]{0:T(128)S(1)} %select_reduce_fusion), channel_id=1, replica_groups=mesh['mp'=2,'vocab'=64,'rows'=2] {'vocab'}, use_global_device_ids=true, to_apply=%region_8.9 | all-reduce | flops 256 | bytes 2048 | tf_op jit(solution)/shard_map/psum | solution.py:85
  572.5 2.7 broadcast_subtract_fusion
  575.2 2.3 copy.43
  (35 shorter events, 9.1 us)
Async XLA Ops:
  7.2 430.3 %copy-start = (bf16[4,512,512]{2,1,0:T(8,128)(2,1)S(1)}, bf16[4,512,512]{2,1,0:T(8,128)(2,1)}, u32[]{:S(2)}) copy-start(bf16[4,512,512]{2,1,0:T(8,128)(2,1)} %param.14) | copy-start | bytes 6291460
  7.2 78.9 %reduce-scatter.2.cloned.1.call-start = ((), (), s32[]{:S(2)}) async-start(), calls=%async_computation.4 | async-start | bytes 4718592 | tf_op jit(solution)/shard_map/reduce_scatter | solution.py:41
  16.2 2.8 slice-start
  18.5 1.7 slice-start.1
  89.2 275.0 %collective-permute-start.1 = (f32[2,128,1536]{1,2,0:T(8,128)}, f32[2,128,1536]{1,2,0:T(8,128)}, u32[]{:S(2)}, u32[]{:S(2)}) collective-permute-start(f32[2,128,1536]{1,2,0:T(8,128)} %copy.37), channel_id=1, source_target_pairs={{2,0},{4,2},{6,4},{8,6},{10,8},{12,10},{14,12},{16,14},{18,16},{20... | collective-permute-start | bytes 4718600 | tf_op jit(solution)/shard_map/ppermute | solution.py:15
  91.7 272.4 %collective-permute-start = (f32[2,128,1536]{1,2,0:T(8,128)}, f32[2,128,1536]{1,2,0:T(8,128)}, u32[]{:S(2)}, u32[]{:S(2)}) collective-permute-start(f32[2,128,1536]{1,2,0:T(8,128)} %copy.37), channel_id=1, source_target_pairs={{0,2},{2,4},{4,6},{6,8},{8,10},{10,12},{12,14},{14,16},{16,18},{18... | collective-permute-start | bytes 4718600 | tf_op jit(solution)/shard_map/ppermute | solution.py:12
  361.0 8.0 %all-to-all-start.1 = ((f32[2,1,128]{2,1,0:T(1,128)}), f32[2,1,128]{2,1,0:T(1,128)S(1)}, u32[]{:S(2)}, u32[]{:S(2)}) async-start(f32[2,1,128]{2,1,0:T(1,128)} %bitcast.10), calls=%async_computation.2 | async-start | bytes 2048 | tf_op jit(solution)/shard_map/all_to_all | solution.py:57
  369.0 6.8 %copy-start.2 = (s32[4]{0:T(128)S(1)}, s32[4]{0:T(128)}, u32[]{:S(2)}) copy-start(s32[4]{0:T(128)} %param.11) | copy-start | bytes 52
  369.0 6.9 %copy-start.3 = (s32[4]{0:T(128)S(1)}, s32[4]{0:T(128)}, u32[]{:S(2)}) copy-start(s32[4]{0:T(128)} %param.12) | copy-start | bytes 52
  369.0 57.0 %all-to-all-start = ((f32[2,128,4608]{1,2,0:T(8,128)}), f32[2,128,4608]{1,2,0:T(8,128)}, u32[]{:S(2)}, u32[]{:S(2)}) async-start(f32[2,128,4608]{1,2,0:T(8,128)} %pad_maximum_fusion), calls=%async_computation.1 | async-start | bytes 9437184 | tf_op jit(solution)/shard_map/all_to_all | solution.py:56
  439.0 4.7 copy-start.1
Sparse Core Ops, SparseCore 0:
  31.9 54.1 reduce-scatter.1
where the time goes:
time: 585 us; the launch traced here: 584 us
  blocking collectives  395 us (68%)
  waiting for transfers between devices  104 us (18%)
  other arithmetic  20.5 us (4%)
  local copies, waits for them, and re-layouts  17.9 us (3%)
  matrix products  16.2 us (3%)
  starting transfers between devices  15 us (3%)
  between operations  14.9 us (3%)
    pmax x1, blocking collectives, on_device(): row_peak = lax.pmax(jnp.max(logits, axis=1), 'vocab')  134 us
    psum x1, blocking collectives, on_device(): row_mass, picked = lax.psum((jnp.sum(mapped, axis=1), picked), 'vocab')  126 us
    psum x1, blocking collectives, on_device(): lax.psum(jnp.sum(jnp.exp(logits - row_peak[:, None]), axis=1), 'vocab')  124 us
    reduce_scatter x1, waiting for transfers between devices, on_device(): lax.psum_scatter(jnp.dot(normed, head_wide, preferred_element_type=jnp.fl...  54.3 us
    all_to_all x1, waiting for transfers between devices, on_device(): lax.all_to_all(padded, 'mp', split_axis=0, concat_axis=0, tiled=True)  50.1 us
  transfers between devices with their start and end apart: 5, of which 2 were waited for; matrix products, arithmetic and copies ran while one was open for 1% of the time, Pallas kernels for 0%

commit v1 on v0

v1 whole, which is shorter than its diff:
```python
import functools

import jax
import jax.numpy as jnp
from jax import lax
from jax.experimental import pallas as pl
from jax.experimental.pallas import tpu as pltpu
from jax.sharding import PartitionSpec as P

MESH = pl.DeviceIdType.MESH
NX, NZ, NC = 4, 8, 2
Q = 128
CW = 256
BLOCK = 512
NCH = 6
NB = 3
FEAT = 2048
FLOOR = 1.9287498479639178e-22


def kernel(
    hid, gain, head, psrc, ptgt, pcnt, wts, ntok,
    out, nll,
    xraw, x2, g_buf, hb, wb, snd, sndm, rcv, rcvm, own, el, ql, pq, pm, mp_buf, st, part_st, all_st,
    ld_sem, hd_sem, ys, yr, yms, ymr, hs, hr, hms, hmr, cs, as_, ar,
):
    m = lax.axis_index("mp")
    v = lax.axis_index("vocab")
    r = lax.axis_index("rows")
    x, z, c = v // (NZ * NC), lax.rem(v // NC, NZ), lax.rem(v, NC)
    v_up, v_down = lax.rem(v + 1, 64), lax.rem(v + 63, 64)

    peers = [(1 - m, v, r), (1 - m, v, 1 - r), (m, v, 1 - r)]
    quarters = [(1 - m) * 2 + r, (1 - m) * 2 + 1 - r, m * 2 + 1 - r, m * 2 + r]
    core_peer = (m, (x * NZ + z) * NC + 1 - c, r)

    def far(dx, dz):
        return (m, (lax.rem(x + dx, NX) * NZ + lax.rem(z + dz, NZ)) * NC + c, r)

    offsets = [(dx, dz) for dx in range(NX) for dz in range(NZ) if dx or dz]

    c_hid = pltpu.make_async_copy(hid.at[0], xraw, ld_sem.at[0])
    c_gain = pltpu.make_async_copy(gain, g_buf, ld_sem.at[1])
    c_w = pltpu.make_async_copy(wts, wb, ld_sem.at[2])
    c_hid.start()
    c_gain.start()

    def head_copy(j):
        cols = pl.ds(pl.multiple_of(j * CW, CW), CW)
        return pltpu.make_async_copy(head.at[0, :, cols], hb.at[j], hd_sem.at[j])

    for j in range(NCH):
        head_copy(j).start()
    c_w.start()

    barrier = pltpu.get_barrier_semaphore()
    greet = peers + [(m, v_up, r), (m, v_down, r)] + [far(*o) for o in offsets]
    for d in greet:
        pl.semaphore_signal(barrier, inc=1, device_id=d, device_id_type=MESH)

    rows_i = lax.broadcasted_iota(jnp.int32, (Q, Q), 0)
    cols_i = lax.broadcasted_iota(jnp.int32, (Q, Q), 1)
    eye = rows_i == cols_i

    def to_row(col):
        return jnp.sum(jnp.where(eye, col, 0.0), axis=0, keepdims=True)

    def to_col(row):
        return jnp.sum(jnp.where(eye, row, 0.0), axis=1, keepdims=True)

    c_hid.wait()
    c_gain.wait()
    g = g_buf[...].astype(jnp.float32)
    for k in range(4):
        a = xraw[pl.ds(pl.multiple_of(quarters[k] * Q, Q), Q), :].astype(jnp.float32)
        sq = jnp.sum(a * a, axis=1, keepdims=True)
        if k < 3:
            for j in range(NCH):
                sndm[j, k, 1:2, :] = to_row(sq)
        else:
            own_sq = sq
        a = a * g
        hi = a.astype(jnp.bfloat16)
        x2[k * 2 * Q : k * 2 * Q + Q, :] = hi
        x2[k * 2 * Q + Q : (k + 1) * 2 * Q, :] = (a - hi.astype(jnp.float32)).astype(jnp.bfloat16)

    pl.semaphore_wait(barrier, len(greet))

    def y_copy(j, k):
        return pltpu.make_async_remote_copy(
            src_ref=snd.at[j, k], dst_ref=rcv.at[j, k], send_sem=ys.at[j, k], recv_sem=yr.at[j, k],
            device_id=peers[k], device_id_type=MESH,
        )

    def ym_copy(j, k):
        return pltpu.make_async_remote_copy(
            src_ref=sndm.at[j, k], dst_ref=rcvm.at[j, k], send_sem=yms.at[j, k], recv_sem=ymr.at[j, k],
            device_id=peers[k], device_id_type=MESH,
        )

    def produce(j, carry):
        head_copy(j).wait()
        w = hb[j]
        for k in range(4):
            p2 = jnp.dot(x2[k * 2 * Q : (k + 1) * 2 * Q, :], w, preferred_element_type=jnp.float32)
            p = p2[:Q] + p2[Q:]
            if k == 3:
                own[j] = p
            else:
                top = jnp.maximum(jnp.max(jnp.abs(p), axis=1, keepdims=True), 1e-30)
                snd[j, k] = jnp.round(p * (32767.0 / top)).astype(jnp.int32).astype(jnp.int16)
                y_copy(j, k).start()
                sndm[j, k, 0:1, :] = to_row(top * (1.0 / 32767.0))
                ym_copy(j, k).start()
        return carry

    lax.fori_loop(0, NCH, produce, 0)

    def halo(b):
        copies = []
        for d, (target, slot) in enumerate((((m, v_up, r), b), ((m, v_down, r), 2 * NB + b))):
            copies.append(pltpu.make_async_remote_copy(
                src_ref=pq.at[NB + b], dst_ref=pq.at[slot], send_sem=hs.at[d, b], recv_sem=hr.at[d, b],
                device_id=target, device_id_type=MESH,
            ))
            copies.append(pltpu.make_async_remote_copy(
                src_ref=pm.at[NB + b], dst_ref=pm.at[slot], send_sem=hms.at[d, b], recv_sem=hmr.at[d, b],
                device_id=target, device_id_type=MESH,
            ))
        return copies

    token = to_col(ntok[...].astype(jnp.float32))
    lane = lax.broadcasted_iota(jnp.int32, (Q, BLOCK), 1).astype(jnp.float32)
    scale_own = scale_oth = None
    l_tops, q_tops, l_sums, q_sums = [], [], [], []
    tok_l = jnp.zeros((Q, 1), jnp.float32)
    for b in range(NB):
        for j in (2 * b, 2 * b + 1):
            for k in range(3):
                y_copy(j, k).wait_recv()
                ym_copy(j, k).wait_recv()
            if j == 0:
                sq = [to_col(rcvm[0, k, 1:2, :]) for k in range(3)]
                scale_own = lax.rsqrt((own_sq + sq[2]) * (1.0 / 4096.0) + 1e-05)
                scale_oth = lax.rsqrt((sq[0] + sq[1]) * (1.0 / 4096.0) + 1e-05)
            f = [to_col(rcvm[j, k, 0:1, :]) for k in range(3)]
            half = slice((j % 2) * CW, (j % 2 + 1) * CW)
            mine = own[j] * scale_own + rcv[j, 2].astype(jnp.float32) * (f[2] * scale_own)
            other = rcv[j, 0].astype(jnp.float32) * (f[0] * scale_oth) + rcv[j, 1].astype(
                jnp.float32
            ) * (f[1] * scale_oth)
            ql[m, :, half] = mine
            ql[1 - m, :, half] = other
        qb = ql[1]
        top = jnp.max(qb, axis=1, keepdims=True)
        e = jnp.exp(qb - top)
        pq[NB + b] = e.astype(jnp.bfloat16)
        pm[NB + b] = to_row(top)
        for cp in halo(b):
            cp.start()
        q_tops.append(top)
        q_sums.append(jnp.sum(e, axis=1, keepdims=True))
        lb = ql[0]
        top = jnp.max(lb, axis=1, keepdims=True)
        e = jnp.exp(lb - top)
        el[b] = e
        l_tops.append(top)
        l_sums.append(jnp.sum(e, axis=1, keepdims=True))
        base = ((v * NB + b) * BLOCK).astype(jnp.float32)
        tok_l = tok_l + jnp.sum(jnp.where(lane == token - base, lb, 0.0), axis=1, keepdims=True)

    def combine(tops, sums):
        top = functools.reduce(jnp.maximum, tops)
        return top, sum(s * jnp.exp(t - top) for s, t in zip(sums, tops))

    l_top, l_sum = combine(l_tops, l_sums)
    q_top, q_sum = combine(q_tops, q_sums)

    c_w.wait()
    for b in range(NB):
        for cp in halo(b):
            cp.wait_recv()

    live, target, tops, prods = [], [], [], []
    for s in range(4):
        at = jnp.clip(psrc[s] - (v * NB - NB), 0, 3 * NB - 1)
        alive = (pcnt[0] > s).astype(jnp.float32)
        live.append(alive)
        target.append(ptgt[s] - v * NB)
        tops.append(to_col(pm[at]))
        prods.append(jnp.dot(pq[at], wb[s], preferred_element_type=jnp.float32))
    shift = functools.reduce(
        jnp.maximum, [jnp.where(a > 0.5, t, -jnp.inf) for a, t in zip(live, tops)]
    )
    factors = [
        jnp.where(a > 0.5, jnp.exp(jnp.minimum(t - shift, 0.0)), 0.0) for a, t in zip(live, tops)
    ]
    mass = jnp.zeros((Q, 1), jnp.float32)
    tok_m = jnp.zeros((Q, 1), jnp.float32)
    for t in range(NB):
        total = sum(
            prods[s] * (factors[s] * (target[s] == t).astype(jnp.float32)) for s in range(4)
        )
        mp_buf[t] = total
        mass = mass + jnp.sum(total, axis=1, keepdims=True)
        base = ((v * NB + t) * BLOCK).astype(jnp.float32)
        tok_m = tok_m + jnp.sum(jnp.where(lane == token - base, total, 0.0), axis=1, keepdims=True)

    t_top = jnp.maximum(q_top, shift)
    up = jnp.exp(shift - t_top)
    for i, col in enumerate(
        (t_top, q_sum * jnp.exp(q_top - t_top), mass * up, tok_m * up, l_top, l_sum, tok_l)
    ):
        st[i : i + 1, :] = to_row(col)
    st[7:8, :] = jnp.zeros((1, Q), jnp.float32)

    def merge(rows):
        tq, tl = rows[0], rows[4]
        nq = jnp.max(tq, axis=0, keepdims=True)
        nl = jnp.max(tl, axis=0, keepdims=True)
        eq, e_l = jnp.exp(tq - nq), jnp.exp(tl - nl)

        def add(a):
            return jnp.sum(a, axis=0, keepdims=True)

        return (
            nq, add(rows[1] * eq), add(rows[2] * eq), add(rows[3] * eq), nl, add(rows[5] * e_l), add(rows[6]),
        )

    core = pltpu.make_async_remote_copy(
        src_ref=st, dst_ref=part_st, send_sem=cs.at[0], recv_sem=cs.at[1],
        device_id=core_peer, device_id_type=MESH,
    )
    core.start()
    core.wait_recv()
    pair = [jnp.concatenate([st[i : i + 1, :], part_st[i : i + 1, :]], axis=0) for i in range(7)]
    for i, row in enumerate(merge(pair)):
        all_st[0, i : i + 1, :] = row
    all_st[0, 7:8, :] = jnp.zeros((1, Q), jnp.float32)

    spread = [
        pltpu.make_async_remote_copy(
            src_ref=all_st.at[0], dst_ref=all_st.at[dx * NZ + dz], send_sem=as_.at[dx * NZ + dz],
            recv_sem=ar.at[dx * NZ + dz], device_id=far(dx, dz), device_id_type=MESH,
        )
        for dx, dz in offsets
    ]
    for cp in spread:
        cp.start()
    for cp in spread:
        cp.wait_recv()
    nq, sum_q, sum_m, sum_t, nl, sum_l, t_l = merge([all_st[:, i, :] for i in range(7)])
    lse_l = nl + jnp.log(sum_l)
    log_norm = jnp.log(1.0 + sum_m / sum_q)
    nll[...] = log_norm - jnp.log(
        jnp.maximum(jnp.exp(t_l - lse_l), FLOOR) + sum_t / sum_q
    )
    lse_col = to_col(lse_l)
    norm_col = to_col(log_norm)
    m_fac = jnp.exp(shift - to_col(nq)) / to_col(sum_q)
    for b in range(NB):
        l_fac = jnp.exp(l_tops[b] - lse_col)
        out[:, b * BLOCK : (b + 1) * BLOCK] = (
            jnp.log(jnp.maximum(el[b] * l_fac, FLOOR) + mp_buf[b] * m_fac) - norm_col
        )

    for j in range(NCH):
        for k in range(3):
            y_copy(j, k).wait_send()
            ym_copy(j, k).wait_send()
    for b in range(NB):
        for cp in halo(b):
            cp.wait_send()
    core.wait_send()
    for cp in spread:
        cp.wait_send()


def on_device(
    hidden, norm_gain, head_weights, pair_source, pair_target, pair_count, pair_weight, next_token
):
    hbm = pl.BlockSpec(memory_space=pl.ANY)
    smem = pl.BlockSpec(memory_space=pltpu.SMEM)
    vmem = pl.BlockSpec(memory_space=pltpu.VMEM)
    dma = pltpu.SemaphoreType.DMA
    f32, bf16 = jnp.float32, jnp.bfloat16
    ensemble, nll = pl.pallas_call(
        kernel,
        out_shape=(
            jax.ShapeDtypeStruct((Q, NB * BLOCK), f32),
            jax.ShapeDtypeStruct((1, Q), f32),
        ),
        in_specs=[hbm, hbm, hbm, smem, smem, smem, hbm, vmem],
        out_specs=(vmem, vmem),
        scratch_shapes=[
            pltpu.VMEM((4 * Q, FEAT), bf16),
            pltpu.VMEM((8 * Q, FEAT), bf16),
            pltpu.VMEM((1, FEAT), bf16),
            pltpu.VMEM((NCH, FEAT, CW), bf16),
            pltpu.VMEM((4, BLOCK, BLOCK), bf16),
            pltpu.VMEM((NCH, 3, Q, CW), jnp.int16),
            pltpu.VMEM((NCH, 3, 2, Q), f32),
            pltpu.VMEM((NCH, 3, Q, CW), jnp.int16),
            pltpu.VMEM((NCH, 3, 2, Q), f32),
            pltpu.VMEM((NCH, Q, CW), f32),
            pltpu.VMEM((NB, Q, BLOCK), f32),
            pltpu.VMEM((2, Q, BLOCK), f32),
            pltpu.VMEM((3 * NB, Q, BLOCK), bf16),
            pltpu.VMEM((3 * NB, 1, Q), f32),
            pltpu.VMEM((NB, Q, BLOCK), f32),
            pltpu.VMEM((8, Q), f32),
            pltpu.VMEM((8, Q), f32),
            pltpu.VMEM((NX * NZ, 8, Q), f32),
            dma((3,)),
            dma((NCH,)),
            dma((NCH, 3)),
            dma((NCH, 3)),
            dma((NCH, 3)),
            dma((NCH, 3)),
            dma((2, NB)),
            dma((2, NB)),
            dma((2, NB)),
            dma((2, NB)),
            dma((2,)),
            dma((NX * NZ,)),
            dma((NX * NZ,)),
        ],
        compiler_params=pltpu.CompilerParams(
            collective_id=0, has_side_effects=True, vmem_limit_bytes=48 * 2**20
        ),
        cost_estimate=pl.CostEstimate(
            flops=4 * 4 * Q * FEAT * NB * BLOCK, bytes_accessed=12 * 2**20, transcendentals=10**6
        ),
        name="ensemble",
    )(
        hidden, norm_gain, head_weights, pair_source, pair_target, pair_count, pair_weight,
        next_token.reshape(1, Q),
    )
    return ensemble, nll.reshape(Q)


def solution(mesh):
    in_specs = (
        P("mp", None, "rows"),
        P("mp", "rows"),
        P("mp", "rows", "vocab"),
        P("vocab"),
        P("vocab"),
        P("vocab"),
        P("vocab", None, None),
        P(("mp", "rows")),
    )
    out_specs = (P(("mp", "rows"), "vocab"), P(("mp", "rows")))
    return jax.shard_map(
        on_device, mesh=mesh, in_specs=in_specs, out_specs=out_specs, check_vma=False
    )
```

time: 585 us -> 56 us (0.10)
  blocking collectives: 395 us -> 0 us
  waiting for transfers between devices: 104 us -> 0 us
  Pallas kernels: 0 us -> 47.3 us
  other arithmetic: 20.5 us -> 0 us
  matrix products: 16.2 us -> 0 us
  starting transfers between devices: 15 us -> 0 us
  between operations: 14.9 us -> 1.3 us
  local copies, waits for them, and re-layouts: 17.9 us -> 7.23 us
    psum x3 -> x0, blocking collectives: 256 us -> none  [the longest x1 126 us: on_device(): row_mass, picked = lax.psum((jnp.sum(mapped, axis=1), picked), 'vocab')]
    pmax x1 -> x0, blocking collectives: 134 us -> none  [on_device(): row_peak = lax.pmax(jnp.max(logits, axis=1), 'vocab')]
    reduce_scatter x1 -> x0, waiting for transfers between devices: 54.3 us -> none  [on_device(): lax.psum_scatter(jnp.dot(normed, head_wide, preferred_element_type=jnp.fl...]
    all_to_all x2 -> x0, waiting for transfers between devices: 50.1 us -> none  [the longest x1 50.1 us: on_device(): lax.all_to_all(padded, 'mp', split_axis=0, concat_axis=0, tiled=True)]
    pallas_call x0 -> x1, Pallas kernels: none -> 47.3 us  [on_device(): pl.pallas_call(kernel, out_shape=(jax.ShapeDtypeStruct((Q, NB * BLOCK), f...]
    dot_general x3 -> x0, matrix products: 16.2 us -> none  [the longest x1 11.6 us: on_device(): jnp.dot(normed, head_wide, preferred_element_type=jnp.float32, precision=...]
    all_to_all x2 -> x0, starting transfers between devices: 9.32 us -> none  [the longest x1 6.13 us: on_device(): lax.all_to_all(padded, 'mp', split_axis=0, concat_axis=0, tiled=True)]
    squeeze x2 -> x0, local copies, waits for them, and re-layouts: 7.96 us -> none  [the longest x1 4.8 us: on_device(): llama_part = received[0][:, shard_cols:2 * shard_cols]]
  transfers between devices with their start and end apart: 5 -> 0, of which waited for: 2 -> 0; matrix products, arithmetic and copies ran while one was open for 1% -> 0% of each run, Pallas kernels for 0% -> 0%
where the time goes in v1:
time: 56 us; the launch traced here: 55.8 us
  Pallas kernels  47.3 us (84%)
  local copies, waits for them, and re-layouts  7.23 us (13%)
  between operations  1.3 us (2%)
    pallas_call x1, Pallas kernels, on_device(): pl.pallas_call(kernel, out_shape=(jax.ShapeDtypeStruct((Q, NB * BLOCK), f...  47.3 us
    unnamed x14, local copies, waits for them, and re-layouts  7.23 us

profile of v1, /device:TPU:1, one launch (start us, length us, event | category | flops | bytes accessed | tf_op | source)
XLA Modules:
  0.0 55.8 jit_solution(14916174311868638044)
XLA Ops:
  1.3 0.0 copy-start
  1.3 1.6 %copy-done = bf16[1,512,2048]{2,1,0:T(8,128)(2,1)S(1)} copy-done((bf16[1,512,2048]{2,1,0:T(8,128)(2,1)S(1)}, bf16[1,512,2048]{2,1,0:T(8,128)(2,1)}, u32[]{:S(2)}) %copy-start) | copy-done | bytes 2097176
  2.9 0.0 copy-start.1
  2.9 1.6 %copy-done.1 = bf16[4,512,512]{2,1,0:T(8,128)(2,1)S(1)} copy-done((bf16[4,512,512]{2,1,0:T(8,128)(2,1)S(1)}, bf16[4,512,512]{2,1,0:T(8,128)(2,1)}, u32[]{:S(2)}) %copy-start.1) | copy-done | bytes 2097176
  4.5 0.0 copy-start.2
  4.5 0.7 %copy-done.2 = bf16[1,2048]{1,0:T(2,128)(2,1)S(1)} copy-done((bf16[1,2048]{1,0:T(2,128)(2,1)S(1)}, bf16[1,2048]{1,0:T(2,128)(2,1)}, u32[]{:S(2)}) %copy-start.2) | copy-done | bytes 4120
  5.2 0.0 copy-start.3
  5.2 0.7 %copy-done.3 = s32[4]{0:T(128)S(1)} copy-done((s32[4]{0:T(128)S(1)}, s32[4]{0:T(128)}, u32[]{:S(2)}) %copy-start.3) | copy-done | bytes 40
  5.8 0.0 copy-start.4
  5.8 0.7 %copy-done.4 = s32[4]{0:T(128)S(1)} copy-done((s32[4]{0:T(128)S(1)}, s32[4]{0:T(128)}, u32[]{:S(2)}) %copy-start.4) | copy-done | bytes 40
  6.5 0.0 copy-start.5
  6.5 0.7 %copy-done.5 = s32[128]{0:T(128)S(1)} copy-done((s32[128]{0:T(128)S(1)}, s32[128]{0:T(128)}, u32[]{:S(2)}) %copy-start.5) | copy-done | bytes 536
  7.1 47.3 %ensemble.1 = (f32[128,1536]{1,0:T(8,128)S(1)}, f32[1,128]{1,0:T(1,128)S(1)}) custom-call(bf16[1,512,2048]{2,1,0:T(8,128)(2,1)S(1)} %copy-done, bf16[1,2048]{1,0:T(2,128)(2,1)S(1)} %copy-done.2, bf16[1,2048,1536]{2,1,0:T(8,128)(2,1)} %head.1, s32[4]{0:T(128)S(1)} %copy-done.3, s32[4]{0:T(128)S(1)} %copy-done.4, s32[1]{0:T(128)S(6)} %copy.12.pcnt, ...), custom_call_target="tpu_custom_call" | custom-call | flops 6442450944 | bytes 12582912 | tf_op jit(solution)/shard_map/ensemble/pallas_call | solution.py:287
  54.4 0.9 %copy.13 = f32[128,1536]{1,0:T(8,128)} copy(f32[128,1536]{1,0:T(8,128)S(1)} %get-tuple-element.8) | data formatting | bytes 1572864
  55.3 0.5 copy.14
Async XLA Ops:
  1.3 1.6 %copy-start = (bf16[1,512,2048]{2,1,0:T(8,128)(2,1)S(1)}, bf16[1,512,2048]{2,1,0:T(8,128)(2,1)}, u32[]{:S(2)}) copy-start(bf16[1,512,2048]{2,1,0:T(8,128)(2,1)} %hid.1) | copy-start | bytes 6291460
  2.9 1.6 %copy-start.1 = (bf16[4,512,512]{2,1,0:T(8,128)(2,1)S(1)}, bf16[4,512,512]{2,1,0:T(8,128)(2,1)}, u32[]{:S(2)}) copy-start(bf16[4,512,512]{2,1,0:T(8,128)(2,1)} %wts.1) | copy-start | bytes 6291460
  4.5 0.7 %copy-start.2 = (bf16[1,2048]{1,0:T(2,128)(2,1)S(1)}, bf16[1,2048]{1,0:T(2,128)(2,1)}, u32[]{:S(2)}) copy-start(bf16[1,2048]{1,0:T(2,128)(2,1)} %gain.1) | copy-start | bytes 12292
  5.2 0.7 %copy-start.3 = (s32[4]{0:T(128)S(1)}, s32[4]{0:T(128)}, u32[]{:S(2)}) copy-start(s32[4]{0:T(128)} %psrc.1) | copy-start | bytes 52
  5.8 0.7 %copy-start.4 = (s32[4]{0:T(128)S(1)}, s32[4]{0:T(128)}, u32[]{:S(2)}) copy-start(s32[4]{0:T(128)} %ptgt.1) | copy-start | bytes 52
  6.5 0.7 %copy-start.5 = (s32[128]{0:T(128)S(1)}, s32[128]{0:T(128)}, u32[]{:S(2)}) copy-start(s32[128]{0:T(128)} %param.15) | copy-start | bytes 1540

commit v2 on v1

v2 whole, which is shorter than its diff:
```python
import functools

import jax
import jax.numpy as jnp
from jax import lax
from jax.experimental import pallas as pl
from jax.experimental.pallas import tpu as pltpu
from jax.sharding import PartitionSpec as P

MESH = pl.DeviceIdType.MESH
NX, NZ, NC = 4, 8, 2
Q = 128
CW = 256
BLOCK = 512
NCH = 6
NB = 3
FEAT = 2048
FLOOR = 1.9287498479639178e-22


def kernel(
    hid, gain, head, psrc_in, ptgt_in, pcnt_in, wts, ntok_in,
    out, nll,
    psrc, ptgt, pcnt, ntok, xraw, x2, g_buf, hb, wb, snd, sndm, part, rcv, rcvm, own, own_sq, lg, el, pq, pm, q_sums,
    l_tops, l_lse, l_tok, mp_buf, st_q, got_q, all_q, st_l, got_l, all_l,
    ld_sem, hd_sem, ys, yr, yms, ymr, hs, hr, hms, hmr, cs, qss, qsr, lss, lsr,
):
    m = lax.axis_index("mp")
    v = lax.axis_index("vocab")
    r = lax.axis_index("rows")
    x, z, c = v // (NZ * NC), lax.rem(v // NC, NZ), lax.rem(v, NC)
    v_up, v_down = lax.rem(v + 1, 64), lax.rem(v + 63, 64)

    peers = [(1 - m, v, r), (1 - m, v, 1 - r), (m, v, 1 - r)]
    quarters = [(1 - m) * 2 + r, (1 - m) * 2 + 1 - r, m * 2 + 1 - r, m * 2 + r]
    core_peer = (m, (x * NZ + z) * NC + 1 - c, r)

    def far(dx, dz):
        return (m, (lax.rem(x + dx, NX) * NZ + lax.rem(z + dz, NZ)) * NC + c, r)

    offsets = sorted(
        ((dx, dz) for dx in range(NX) for dz in range(NZ) if dx or dz),
        key=lambda o: -min(o[0], NX - o[0]) - min(o[1], NZ - o[1]),
    )

    c_hid = pltpu.make_async_copy(hid.at[0], xraw, ld_sem.at[0])
    c_gain = pltpu.make_async_copy(gain, g_buf, ld_sem.at[1])
    c_w = pltpu.make_async_copy(wts, wb, ld_sem.at[2])
    c_hid.start()
    c_gain.start()

    def head_copy(j):
        cols = pl.ds(pl.multiple_of(j * CW, CW), CW)
        return pltpu.make_async_copy(head.at[0, :, cols], hb.at[j], hd_sem.at[j])

    for j in range(NCH):
        head_copy(j).start()
    c_w.start()
    lists = [
        pltpu.make_async_copy(src, dst, ld_sem.at[3 + i])
        for i, (src, dst) in enumerate(
            ((psrc_in, psrc), (ptgt_in, ptgt), (pcnt_in, pcnt), (ntok_in, ntok))
        )
    ]
    for cp in lists:
        cp.start()

    barrier = pltpu.get_barrier_semaphore()
    greet = peers + [(m, v_up, r), (m, v_down, r)] + [far(*o) for o in offsets]
    for d in greet:
        pl.semaphore_signal(barrier, inc=1, device_id=d, device_id_type=MESH)

    rows_i = lax.broadcasted_iota(jnp.int32, (Q, Q), 0)
    cols_i = lax.broadcasted_iota(jnp.int32, (Q, Q), 1)
    eye = rows_i == cols_i

    def to_row(col):
        return jnp.sum(jnp.where(eye, col, 0.0), axis=0, keepdims=True)

    def to_col(row):
        return jnp.sum(jnp.where(eye, row, 0.0), axis=1, keepdims=True)

    for edge, at in ((v == 0, 0), (v == 63, 2 * NCH)):

        @pl.when(edge)
        def _(at=at):
            pq[at : at + NCH] = jnp.zeros((NCH, Q, CW), jnp.bfloat16)
            pm[at : at + NCH] = jnp.zeros((NCH, 1, Q), jnp.float32)

    c_hid.wait()
    c_gain.wait()
    g = g_buf[...].astype(jnp.float32)
    for k in range(4):
        a = xraw[pl.ds(pl.multiple_of(quarters[k] * Q, Q), Q), :].astype(jnp.float32)
        sq = jnp.sum(a * a, axis=1, keepdims=True)
        if k < 3:
            for j in range(NCH):
                sndm[j, k, 1:2, :] = to_row(sq)
        else:
            own_sq = sq
        a = a * g
        hi = a.astype(jnp.bfloat16)
        x2[k * 2 * Q : k * 2 * Q + Q, :] = hi
        x2[k * 2 * Q + Q : (k + 1) * 2 * Q, :] = (a - hi.astype(jnp.float32)).astype(jnp.bfloat16)

    pl.semaphore_wait(barrier, len(greet))

    def y_copy(j, k):
        return pltpu.make_async_remote_copy(
            src_ref=snd.at[j, k], dst_ref=rcv.at[j, k], send_sem=ys, recv_sem=yr.at[j],
            device_id=peers[k], device_id_type=MESH,
        )

    def ym_copy(j, k):
        return pltpu.make_async_remote_copy(
            src_ref=sndm.at[j, k], dst_ref=rcvm.at[j, k], send_sem=yms, recv_sem=ymr.at[j],
            device_id=peers[k], device_id_type=MESH,
        )

    def multiply(j):
        head_copy(j).wait()
        w = hb[j]
        for k in range(4):
            p2 = jnp.dot(x2[k * 2 * Q : (k + 1) * 2 * Q, :], w, preferred_element_type=jnp.float32)
            p = p2[:Q] + p2[Q:]
            if k == 3:
                own[j] = p
            else:
                part[j % 2, k] = p

    def pack(j):
        for k in range(3):
            p = part[j % 2, k]
            top = jnp.maximum(jnp.max(jnp.abs(p), axis=1, keepdims=True), 1e-30)
            snd[j, k] = jnp.round(p * (32767.0 / top)).astype(jnp.int32).astype(jnp.int16)
            sndm[j, k, 0:1, :] = to_row(top * (1.0 / 32767.0))

    def send(j):
        for k in range(3):
            y_copy(j, k).start()
            ym_copy(j, k).start()

    def wait_all(ref, sem):
        pltpu.make_async_copy(ref, ref, sem).wait()

    multiply(0)
    pack(0)
    send(0)
    for j in range(1, NCH + 1):
        if j < NCH:
            multiply(j)
        if j > 1:
            pack(j - 1)
            send(j - 1)

    has = (v < 63, v > 0)

    def halo(j, d):
        target, slot = (((m, v_up, r), j), ((m, v_down, r), 2 * NCH + j))[d]
        return [
            pltpu.make_async_remote_copy(
                src_ref=buf.at[NCH + j], dst_ref=buf.at[slot], send_sem=send.at[d], recv_sem=recv.at[d],
                device_id=target, device_id_type=MESH,
            )
            for buf, send, recv in ((pq, hs, hr), (pm, hms, hmr))
        ]

    def halo_start(j):
        for d in range(2):

            @pl.when(has[d])
            def _(d=d):
                for cp in halo(j, d):
                    cp.start()

    for cp in lists:
        cp.wait()
    token = to_col(ntok[...].reshape(1, Q).astype(jnp.float32))
    lane = lax.broadcasted_iota(jnp.int32, (Q, BLOCK), 1).astype(jnp.float32)

    def at_token(start, values):
        base = (v * (NB * BLOCK) + start).astype(jnp.float32)
        hit = lane[:, : values.shape[1]] == token - base
        return jnp.sum(jnp.where(hit, values, 0.0), axis=1, keepdims=True)

    scale_own = scale_other = None
    for j in range(NCH):
        wait_all(rcv.at[j], yr.at[j])
        wait_all(rcvm.at[j], ymr.at[j])
        if j == 0:
            sq = [rcvm[0, k, 1:2, :] for k in range(3)]
            scale_own = lax.rsqrt((own_sq[...] + sq[2]) * (1.0 / 4096.0) + 1e-05)
            scale_other = lax.rsqrt((sq[0] + sq[1]) * (1.0 / 4096.0) + 1e-05)
        near, cross, far_term = (
            rcv[j, k].astype(jnp.float32)
            * to_col(rcvm[j, k, 0:1, :] * (scale_own if k == 2 else scale_other))
            for k in range(3)
        )
        lg[m] = own[j] * to_col(scale_own) + far_term
        lg[1 - m] = near + cross
        logits = lg[1]
        top = jnp.max(logits, axis=1, keepdims=True)
        e = jnp.exp(logits - top)
        pq[NCH + j] = e.astype(jnp.bfloat16)
        pm[NCH + j] = to_row(top)
        halo_start(j)
        q_sums[j] = to_row(jnp.sum(e, axis=1, keepdims=True))
        logits = lg[0]
        top = jnp.max(logits, axis=1, keepdims=True)
        e = jnp.exp(logits - top)
        el[j] = e
        l_tops[j] = to_row(top)
        l_lse[j] = to_row(top + jnp.log(jnp.sum(e, axis=1, keepdims=True)))
        l_tok[j] = to_row(at_token(j * CW, logits))

    def add(a):
        return jnp.sum(a, axis=0, keepdims=True)

    def merge_q(top, *sums):
        new = jnp.max(top, axis=0, keepdims=True)
        e = jnp.exp(top - new)
        return (new, *(add(a * e) for a in sums))

    def merge_l(lse, tok):
        new = jnp.max(lse, axis=0, keepdims=True)
        return new + jnp.log(add(jnp.exp(lse - new))), add(tok)

    def core_copy(src, dst, i):
        return pltpu.make_async_remote_copy(
            src_ref=src, dst_ref=dst, send_sem=cs.at[i], recv_sem=cs.at[i + 1],
            device_id=core_peer, device_id_type=MESH,
        )

    def spread(ref, send, recv):
        return [
            pltpu.make_async_remote_copy(
                src_ref=ref.at[0], dst_ref=ref.at[dx * NZ + dz], send_sem=send,
                recv_sem=recv, device_id=far(dx, dz), device_id_type=MESH,
            )
            for dx, dz in offsets
        ]

    def both(a, b, i):
        return jnp.concatenate([a[i : i + 1, :], b[i : i + 1, :]], axis=0)

    for i, row in enumerate(merge_l(
        jnp.concatenate([l_lse[j] for j in range(NCH)], axis=0),
        jnp.concatenate([l_tok[j] for j in range(NCH)], axis=0),
    )):
        st_l[i : i + 1, :] = row
    core_l = core_copy(st_l, got_l, 2)
    core_l.start()
    core_l.wait_recv()
    for i, row in enumerate(merge_l(*(both(st_l, got_l, i) for i in range(2)))):
        all_l[0, i : i + 1, :] = row
    spread_l = spread(all_l, lss, lsr)
    for cp in spread_l:
        cp.start()
    c_w.wait()

    for d in range(2):

        @pl.when(has[1 - d])
        def _(d=d):
            slots = pl.ds(2 * NCH * d, NCH)
            wait_all(pq.at[slots], hr.at[d])
            wait_all(pm.at[slots], hmr.at[d])


    live, target, tops, prods = [], [], [], []
    for s in range(4):
        at = 2 * jnp.clip(psrc[s] - (v * NB - NB), 0, 3 * NB - 1)
        for h in range(2):
            live.append((pcnt[0] > s).astype(jnp.float32))
            target.append(ptgt[s] - v * NB)
            tops.append(pm[at + h])
            prods.append(jnp.dot(
                pq[at + h], wb[s, h * CW : (h + 1) * CW, :], preferred_element_type=jnp.float32
            ))
    shift = functools.reduce(
        jnp.maximum, [jnp.where(a > 0.5, t, -jnp.inf) for a, t in zip(live, tops)]
    )
    factors = [
        to_col(jnp.where(a > 0.5, jnp.exp(jnp.minimum(t - shift, 0.0)), 0.0))
        for a, t in zip(live, tops)
    ]
    mass = jnp.zeros((Q, 1), jnp.float32)
    tok_m = jnp.zeros((Q, 1), jnp.float32)
    for t in range(NB):
        total = sum(
            prods[s] * (factors[s] * (target[s] == t).astype(jnp.float32)) for s in range(8)
        )
        mp_buf[t] = total
        mass = mass + jnp.sum(total, axis=1, keepdims=True)
        tok_m = tok_m + at_token(t * BLOCK, total)

    top, q_sum = merge_q(
        jnp.concatenate([pm[NCH + j] for j in range(NCH)], axis=0),
        jnp.concatenate([q_sums[j] for j in range(NCH)], axis=0),
    )
    t_top = jnp.maximum(top, shift)
    up = jnp.exp(shift - t_top)
    for i, row in enumerate((t_top, q_sum * jnp.exp(top - t_top), to_row(mass) * up, to_row(tok_m) * up)):
        st_q[i : i + 1, :] = row
    core_q = core_copy(st_q, got_q, 0)
    core_q.start()
    core_q.wait_recv()
    for i, row in enumerate(merge_q(*(both(st_q, got_q, i) for i in range(4)))):
        all_q[0, i : i + 1, :] = row
    spread_q = spread(all_q, qss, qsr)
    for cp in spread_q:
        cp.start()

    wait_all(snd, ys)
    wait_all(sndm, yms)
    for d in range(2):

        @pl.when(has[d])
        def _(d=d):
            wait_all(pq.at[pl.ds(NCH, NCH)], hs.at[d])
            wait_all(pm.at[pl.ds(NCH, NCH)], hms.at[d])

    core_q.wait_send()
    core_l.wait_send()
    others = pl.ds(1, NX * NZ - 1)
    wait_all(all_q.at[others], qss)
    wait_all(all_l.at[others], lss)
    wait_all(all_q.at[others], qsr)
    nq, sum_q, sum_m, sum_t = merge_q(*(all_q[:, i, :] for i in range(4)))
    log_norm = jnp.log(1.0 + sum_m / sum_q)
    norm_col = to_col(log_norm)
    m_fac = to_col(jnp.exp(shift - nq) / sum_q)
    wait_all(all_l.at[others], lsr)
    lse_l, t_l = merge_l(*(all_l[:, i, :] for i in range(2)))
    nll[...] = log_norm - jnp.log(jnp.maximum(jnp.exp(t_l - lse_l), FLOOR) + sum_t / sum_q)
    for j in range(NCH):
        l_fac = to_col(jnp.exp(l_tops[j] - lse_l))
        mapped = mp_buf[j // 2, :, (j % 2) * CW : (j % 2 + 1) * CW]
        out[:, j * CW : (j + 1) * CW] = (
            jnp.log(jnp.maximum(el[j] * l_fac, FLOOR) + mapped * m_fac) - norm_col
        )


def on_device(
    hidden, norm_gain, head_weights, pair_source, pair_target, pair_count, pair_weight, next_token
):
    hbm = pl.BlockSpec(memory_space=pltpu.HBM)
    vmem = pl.BlockSpec(memory_space=pltpu.VMEM)
    dma = pltpu.SemaphoreType.DMA
    f32, bf16 = jnp.float32, jnp.bfloat16
    ensemble, nll = pl.pallas_call(
        kernel,
        out_shape=(
            pltpu.VMEM((Q, NB * BLOCK), f32),
            pltpu.VMEM((1, Q), f32),
        ),
        in_specs=[pl.BlockSpec(memory_space=pl.ANY)] * 8,
        out_specs=(vmem, vmem),
        scratch_shapes=[
            pltpu.SMEM((4,), jnp.int32),
            pltpu.SMEM((4,), jnp.int32),
            pltpu.SMEM((1,), jnp.int32),
            pltpu.VMEM((Q,), jnp.int32),
            pltpu.VMEM((4 * Q, FEAT), bf16),
            pltpu.VMEM((8 * Q, FEAT), bf16),
            pltpu.VMEM((1, FEAT), bf16),
            pltpu.VMEM((NCH, FEAT, CW), bf16),
            pltpu.VMEM((4, BLOCK, BLOCK), bf16),
            pltpu.VMEM((NCH, 3, Q, CW), jnp.int16),
            pltpu.VMEM((NCH, 3, 2, Q), f32),
            pltpu.VMEM((2, 3, Q, CW), f32),
            pltpu.VMEM((NCH, 3, Q, CW), jnp.int16),
            pltpu.VMEM((NCH, 3, 2, Q), f32),
            pltpu.VMEM((NCH, Q, CW), f32),
            pltpu.VMEM((1, Q), f32),
            pltpu.VMEM((2, Q, CW), f32),
            pltpu.VMEM((NCH, Q, CW), f32),
            pltpu.VMEM((3 * NCH, Q, CW), bf16),
            pltpu.VMEM((3 * NCH, 1, Q), f32),
            pltpu.VMEM((NCH, 1, Q), f32),
            pltpu.VMEM((NCH, 1, Q), f32),
            pltpu.VMEM((NCH, 1, Q), f32),
            pltpu.VMEM((NCH, 1, Q), f32),
            pltpu.VMEM((NB, Q, BLOCK), f32),
            pltpu.VMEM((4, Q), f32),
            pltpu.VMEM((4, Q), f32),
            pltpu.VMEM((NX * NZ, 4, Q), f32),
            pltpu.VMEM((2, Q), f32),
            pltpu.VMEM((2, Q), f32),
            pltpu.VMEM((NX * NZ, 2, Q), f32),
            dma((7,)),
            dma((NCH,)),
            dma(()),
            dma((NCH,)),
            dma(()),
            dma((NCH,)),
            dma((2,)),
            dma((2,)),
            dma((2,)),
            dma((2,)),
            dma((4,)),
            dma(()),
            dma(()),
            dma(()),
            dma(()),
        ],
        compiler_params=pltpu.CompilerParams(
            collective_id=0, has_side_effects=True, vmem_limit_bytes=40 * 2**20
        ),
        cost_estimate=pl.CostEstimate(
            flops=4 * 4 * Q * FEAT * NB * BLOCK, bytes_accessed=12 * 2**20, transcendentals=10**6
        ),
        name="ensemble",
    )(
        *(a if a.shape == (1,) else pltpu.with_memory_space_constraint(a, pltpu.HBM) for a in (
            hidden, norm_gain, head_weights, pair_source, pair_target, pair_count, pair_weight,
            next_token,
        ))
    )
    return ensemble, nll.reshape(Q)


def solution(mesh):
    in_specs = (
        P("mp", None, "rows"),
        P("mp", "rows"),
        P("mp", "rows", "vocab"),
        P("vocab"),
        P("vocab"),
        P("vocab"),
        P("vocab", None, None),
        P(("mp", "rows")),
    )
    out_specs = (P(("mp", "rows"), "vocab"), P(("mp", "rows")))
    return jax.shard_map(
        on_device, mesh=mesh, in_specs=in_specs, out_specs=out_specs, check_vma=False
    )
```

time: 56 us -> 46.1 us (0.82)
  local copies, waits for them, and re-layouts: 7.23 us -> 1.39 us
  Pallas kernels: 47.3 us -> 43.4 us
    unnamed x14 -> x2, local copies, waits for them, and re-layouts: 7.23 us -> 1.39 us
    pallas_call x1, Pallas kernels: 47.3 us -> 43.4 us  [on_device(): pl.pallas_call(kernel, out_shape=(pltpu.VMEM((Q, NB * BLOCK), f32), pltpu...]
where the time goes in v2:
time: 46.1 us; the launch traced here: 46 us
  Pallas kernels  43.4 us (94%)
  local copies, waits for them, and re-layouts  1.39 us (3%)
  between operations  1.29 us (3%)
    pallas_call x1, Pallas kernels, on_device(): pl.pallas_call(kernel, out_shape=(pltpu.VMEM((Q, NB * BLOCK), f32), pltpu...  43.4 us
    unnamed x2, local copies, waits for them, and re-layouts  1.39 us

profile of v2, /device:TPU:1, one launch (start us, length us, event | category | flops | bytes accessed | tf_op | source)
XLA Modules:
  0.0 46.0 jit_solution(5432033018827625029)
XLA Ops:
  1.3 43.4 %ensemble.1 = (f32[128,1536]{1,0:T(8,128)S(1)}, f32[1,128]{1,0:T(1,128)S(1)}) custom-call(bf16[1,512,2048]{2,1,0:T(8,128)(2,1)} %hid.1, bf16[1,2048]{1,0:T(2,128)(2,1)} %gain.1, bf16[1,2048,1536]{2,1,0:T(8,128)(2,1)} %head.1, s32[4]{0:T(128)} %psrc_in.1, s32[4]{0:T(128)} %ptgt_in.1, s32[1]{0:T(128)S(6)} %copy.14.pcnt_in, bf16[4,512,512]{2,1,0:T(8,128)(2,1)} %wts.1, ...), custom_call_target="tpu_custom_call" | custom-call | flops 6442450944 | bytes 12582912 | tf_op jit(solution)/shard_map/ensemble/pallas_call | solution.py:351
  44.7 0.9 %copy.12 = f32[128,1536]{1,0:T(8,128)} copy(f32[128,1536]{1,0:T(8,128)S(1)} %get-tuple-element.6) | data formatting | bytes 1572864
  45.5 0.5 %copy.13 = f32[128]{0:T(128)} copy(f32[128]{0:T(128)S(1)} %bitcast.1) | data formatting | bytes 1024

commit v3 on v2

--- a/solution.py
+++ b/solution.py
@@ -20,10 +20,10 @@
 
 def kernel(
     hid, gain, head, psrc_in, ptgt_in, pcnt_in, wts, ntok_in,
-    out, nll,
-    psrc, ptgt, pcnt, ntok, xraw, x2, g_buf, hb, wb, snd, sndm, part, rcv, rcvm, own, own_sq, lg, el, pq, pm, q_sums,
-    l_tops, l_lse, l_tok, mp_buf, st_q, got_q, all_q, st_l, got_l, all_l,
-    ld_sem, hd_sem, ys, yr, yms, ymr, hs, hr, hms, hmr, cs, qss, qsr, lss, lsr,
+    el, mp_buf, l_fac, m_fac, norm_out, nll,
+    psrc, ptgt, pcnt, ntok, xraw, x2, g_buf, hb, wb, snd, sndm, part, rcv, rcvm, own, own_sq, lg, pq, pm, q_sums,
+    l_tops, l_lse, l_tok, st_q, got_q, all_q, all_t, st_l, got_l, all_l,
+    ld_sem, hid_sem, hd_sem, ys, yr, yms, ymr, hs, hr, hms, hmr, cs, qss, qsr, lss, lsr, tss, tsr,
 ):
     m = lax.axis_index("mp")
     v = lax.axis_index("vocab")
@@ -43,19 +43,21 @@
         key=lambda o: -min(o[0], NX - o[0]) - min(o[1], NZ - o[1]),
     )
 
-    c_hid = pltpu.make_async_copy(hid.at[0], xraw, ld_sem.at[0])
+    def hid_copy(k):
+        at = pl.ds(pl.multiple_of(quarters[k] * Q, Q), Q)
+        return pltpu.make_async_copy(hid.at[0, at], xraw.at[k], hid_sem.at[k])
+
     c_gain = pltpu.make_async_copy(gain, g_buf, ld_sem.at[1])
     c_w = pltpu.make_async_copy(wts, wb, ld_sem.at[2])
-    c_hid.start()
     c_gain.start()
+    for k in range(4):
+        hid_copy(k).start()
 
     def head_copy(j):
         cols = pl.ds(pl.multiple_of(j * CW, CW), CW)
         return pltpu.make_async_copy(head.at[0, :, cols], hb.at[j], hd_sem.at[j])
 
-    for j in range(NCH):
-        head_copy(j).start()
-    c_w.start()
+    head_copy(0).start()
     lists = [
         pltpu.make_async_copy(src, dst, ld_sem.at[3 + i])
         for i, (src, dst) in enumerate(
@@ -87,23 +89,27 @@
             pq[at : at + NCH] = jnp.zeros((NCH, Q, CW), jnp.bfloat16)
             pm[at : at + NCH] = jnp.zeros((NCH, 1, Q), jnp.float32)
 
-    c_hid.wait()
     c_gain.wait()
+    for k in range(4):
+        hid_copy(k).wait()
+    for j in range(1, NCH):
+        head_copy(j).start()
+    c_w.start()
     g = g_buf[...].astype(jnp.float32)
-    for k in range(4):
-        a = xraw[pl.ds(pl.multiple_of(quarters[k] * Q, Q), Q), :].astype(jnp.float32)
-        sq = jnp.sum(a * a, axis=1, keepdims=True)
-        if k < 3:
-            for j in range(NCH):
-                sndm[j, k, 1:2, :] = to_row(sq)
-        else:
-            own_sq = sq
-        a = a * g
+
+    def prepare(k):
+        a = xraw[k].astype(jnp.float32) * g
         hi = a.astype(jnp.bfloat16)
         x2[k * 2 * Q : k * 2 * Q + Q, :] = hi
         x2[k * 2 * Q + Q : (k + 1) * 2 * Q, :] = (a - hi.astype(jnp.float32)).astype(jnp.bfloat16)
 
-    pl.semaphore_wait(barrier, len(greet))
+    def squares(k):
+        a = xraw[k].astype(jnp.float32)
+        sq = to_row(jnp.sum(a * a, axis=1, keepdims=True))
+        if k < 3:
+            sndm[1, k, 1:2, :] = sq
+        else:
+            own_sq[...] = sq
 
     def y_copy(j, k):
         return pltpu.make_async_remote_copy(
@@ -117,16 +123,13 @@
             device_id=peers[k], device_id_type=MESH,
         )
 
-    def multiply(j):
-        head_copy(j).wait()
-        w = hb[j]
-        for k in range(4):
-            p2 = jnp.dot(x2[k * 2 * Q : (k + 1) * 2 * Q, :], w, preferred_element_type=jnp.float32)
-            p = p2[:Q] + p2[Q:]
-            if k == 3:
-                own[j] = p
-            else:
-                part[j % 2, k] = p
+    def multiply(j, k):
+        p2 = jnp.dot(x2[k * 2 * Q : (k + 1) * 2 * Q, :], hb[j], preferred_element_type=jnp.float32)
+        p = p2[:Q] + p2[Q:]
+        if k == 3:
+            own[j] = p
+        else:
+            part[j % 2, k] = p
 
     def pack(j):
         for k in range(3):
@@ -136,20 +139,37 @@
             sndm[j, k, 0:1, :] = to_row(top * (1.0 / 32767.0))
 
     def send(j):
+        for k in (2, 0, 1):
+            y_copy(j, k).start()
         for k in range(3):
-            y_copy(j, k).start()
             ym_copy(j, k).start()
 
     def wait_all(ref, sem):
         pltpu.make_async_copy(ref, ref, sem).wait()
 
-    multiply(0)
+    head_copy(0).wait()
+    for k in range(3):
+        prepare(k)
+        multiply(0, k)
     pack(0)
+    pl.semaphore_wait(barrier, len(greet))
     send(0)
-    for j in range(1, NCH + 1):
+    prepare(3)
+    head_copy(1).wait()
+    for k in range(3):
+        multiply(1, k)
+    for k in range(4):
+        squares(k)
+    pack(1)
+    send(1)
+    multiply(0, 3)
+    multiply(1, 3)
+    for j in range(2, NCH + 1):
         if j < NCH:
-            multiply(j)
-        if j > 1:
+            head_copy(j).wait()
+            for k in range(4):
+                multiply(j, k)
+        if j > 2:
             pack(j - 1)
             send(j - 1)
 
@@ -186,9 +206,11 @@
     scale_own = scale_other = None
     for j in range(NCH):
         wait_all(rcv.at[j], yr.at[j])
-        wait_all(rcvm.at[j], ymr.at[j])
+        if j != 1:
+            wait_all(rcvm.at[j], ymr.at[j])
         if j == 0:
-            sq = [rcvm[0, k, 1:2, :] for k in range(3)]
+            wait_all(rcvm.at[1], ymr.at[1])
+            sq = [rcvm[1, k, 1:2, :] for k in range(3)]
             scale_own = lax.rsqrt((own_sq[...] + sq[2]) * (1.0 / 4096.0) + 1e-05)
             scale_other = lax.rsqrt((sq[0] + sq[1]) * (1.0 / 4096.0) + 1e-05)
         near, cross, far_term = (
@@ -216,14 +238,12 @@
     def add(a):
         return jnp.sum(a, axis=0, keepdims=True)
 
-    def merge_q(top, *sums):
-        new = jnp.max(top, axis=0, keepdims=True)
-        e = jnp.exp(top - new)
-        return (new, *(add(a * e) for a in sums))
+    def log_add(rows):
+        top = jnp.max(rows, axis=0, keepdims=True)
+        return top + jnp.log(add(jnp.exp(rows - top)))
 
     def merge_l(lse, tok):
-        new = jnp.max(lse, axis=0, keepdims=True)
-        return new + jnp.log(add(jnp.exp(lse - new))), add(tok)
+        return log_add(lse), add(tok)
 
     def core_copy(src, dst, i):
         return pltpu.make_async_remote_copy(
@@ -294,21 +314,24 @@
         mass = mass + jnp.sum(total, axis=1, keepdims=True)
         tok_m = tok_m + at_token(t * BLOCK, total)
 
-    top, q_sum = merge_q(
-        jnp.concatenate([pm[NCH + j] for j in range(NCH)], axis=0),
-        jnp.concatenate([q_sums[j] for j in range(NCH)], axis=0),
-    )
-    t_top = jnp.maximum(top, shift)
-    up = jnp.exp(shift - t_top)
-    for i, row in enumerate((t_top, q_sum * jnp.exp(top - t_top), to_row(mass) * up, to_row(tok_m) * up)):
+    lse_q = log_add(jnp.concatenate(
+        [pm[NCH + j] + jnp.log(q_sums[j]) for j in range(NCH)], axis=0
+    ))
+    tok_row = to_row(tok_m)
+    tok_log = jnp.where(tok_row > 0.0, shift + jnp.log(jnp.maximum(tok_row, 1e-37)), -1e30)
+    for i, row in enumerate((lse_q, shift + jnp.log(to_row(mass)), tok_log)):
         st_q[i : i + 1, :] = row
     core_q = core_copy(st_q, got_q, 0)
     core_q.start()
     core_q.wait_recv()
-    for i, row in enumerate(merge_q(*(both(st_q, got_q, i) for i in range(4)))):
-        all_q[0, i : i + 1, :] = row
+    for i in range(2):
+        all_q[0, i : i + 1, :] = log_add(both(st_q, got_q, i))
     spread_q = spread(all_q, qss, qsr)
     for cp in spread_q:
+        cp.start()
+    all_t[0] = log_add(both(st_q, got_q, 2))
+    spread_t = spread(all_t, tss, tsr)
+    for cp in spread_t:
         cp.start()
 
     wait_all(snd, ys)
@@ -325,20 +348,43 @@
     others = pl.ds(1, NX * NZ - 1)
     wait_all(all_q.at[others], qss)
     wait_all(all_l.at[others], lss)
-    wait_all(all_q.at[others], qsr)
-    nq, sum_q, sum_m, sum_t = merge_q(*(all_q[:, i, :] for i in range(4)))
-    log_norm = jnp.log(1.0 + sum_m / sum_q)
-    norm_col = to_col(log_norm)
-    m_fac = to_col(jnp.exp(shift - nq) / sum_q)
+    wait_all(all_t.at[others], tss)
     wait_all(all_l.at[others], lsr)
     lse_l, t_l = merge_l(*(all_l[:, i, :] for i in range(2)))
-    nll[...] = log_norm - jnp.log(jnp.maximum(jnp.exp(t_l - lse_l), FLOOR) + sum_t / sum_q)
     for j in range(NCH):
-        l_fac = to_col(jnp.exp(l_tops[j] - lse_l))
-        mapped = mp_buf[j // 2, :, (j % 2) * CW : (j % 2 + 1) * CW]
-        out[:, j * CW : (j + 1) * CW] = (
-            jnp.log(jnp.maximum(el[j] * l_fac, FLOOR) + mapped * m_fac) - norm_col
-        )
+        l_fac[j] = jnp.exp(l_tops[j] - lse_l)
+    wait_all(all_q.at[others], qsr)
+    total_q, mass_q = (log_add(all_q[:, i, :]) for i in range(2))
+    log_norm = jnp.log(1.0 + jnp.exp(mass_q - total_q))
+    norm_out[...] = log_norm
+    m_fac[...] = jnp.exp(shift - total_q)
+    wait_all(all_t.at[others], tsr)
+    nll[...] = log_norm - jnp.log(
+        jnp.maximum(jnp.exp(t_l - lse_l), FLOOR) + jnp.exp(log_add(all_t[:, 0, :]) - total_q)
+    )
+
+
+def finish(el, mp_buf, l_fac, m_fac, norm_out, nll_in, out, nll, buf, sem):
+    rows_i = lax.broadcasted_iota(jnp.int32, (Q, Q), 0)
+    cols_i = lax.broadcasted_iota(jnp.int32, (Q, Q), 1)
+
+    def to_col(row):
+        return jnp.sum(jnp.where(rows_i == cols_i, row, 0.0), axis=1, keepdims=True)
+
+    copies = [pltpu.make_async_copy(nll_in, nll, sem.at[NCH])]
+    copies[0].start()
+    norm_col, m_col = to_col(norm_out[...]), to_col(m_fac[...])
+    for j in range(NCH):
+        at = slice((j % 2) * CW, (j % 2 + 1) * CW)
+        mapped = mp_buf[j // 2, :, at]
+        buf[:, j * CW : (j + 1) * CW] = (
+            jnp.log(jnp.maximum(el[j] * to_col(l_fac[j]), FLOOR) + mapped * m_col) - norm_col
+        )
+        cols = pl.ds(j * CW, CW)
+        copies.append(pltpu.make_async_copy(buf.at[:, cols], out.at[:, cols], sem.at[j]))
+        copies[-1].start()
+    for cp in copies:
+        cp.wait()
 
 
 def on_device(
@@ -348,20 +394,24 @@
     vmem = pl.BlockSpec(memory_space=pltpu.VMEM)
     dma = pltpu.SemaphoreType.DMA
     f32, bf16 = jnp.float32, jnp.bfloat16
-    ensemble, nll = pl.pallas_call(
+    parts = pl.pallas_call(
         kernel,
         out_shape=(
-            pltpu.VMEM((Q, NB * BLOCK), f32),
+            pltpu.VMEM((NCH, Q, CW), f32),
+            pltpu.VMEM((NB, Q, BLOCK), f32),
+            pltpu.VMEM((NCH, 1, Q), f32),
+            pltpu.VMEM((1, Q), f32),
+            pltpu.VMEM((1, Q), f32),
             pltpu.VMEM((1, Q), f32),
         ),
         in_specs=[pl.BlockSpec(memory_space=pl.ANY)] * 8,
-        out_specs=(vmem, vmem),
+        out_specs=(vmem,) * 6,
         scratch_shapes=[
             pltpu.SMEM((4,), jnp.int32),
             pltpu.SMEM((4,), jnp.int32),
             pltpu.SMEM((1,), jnp.int32),
             pltpu.VMEM((Q,), jnp.int32),
-            pltpu.VMEM((4 * Q, FEAT), bf16),
+            pltpu.VMEM((4, Q, FEAT), bf16),
             pltpu.VMEM((8 * Q, FEAT), bf16),
             pltpu.VMEM((1, FEAT), bf16),
             pltpu.VMEM((NCH, FEAT, CW), bf16),
@@ -374,21 +424,21 @@
             pltpu.VMEM((NCH, Q, CW), f32),
             pltpu.VMEM((1, Q), f32),
             pltpu.VMEM((2, Q, CW), f32),
-            pltpu.VMEM((NCH, Q, CW), f32),
             pltpu.VMEM((3 * NCH, Q, CW), bf16),
             pltpu.VMEM((3 * NCH, 1, Q), f32),
             pltpu.VMEM((NCH, 1, Q), f32),
             pltpu.VMEM((NCH, 1, Q), f32),
             pltpu.VMEM((NCH, 1, Q), f32),
             pltpu.VMEM((NCH, 1, Q), f32),
-            pltpu.VMEM((NB, Q, BLOCK), f32),
             pltpu.VMEM((4, Q), f32),
             pltpu.VMEM((4, Q), f32),
-            pltpu.VMEM((NX * NZ, 4, Q), f32),
+            pltpu.VMEM((NX * NZ, 2, Q), f32),
+            pltpu.VMEM((NX * NZ, 1, Q), f32),
             pltpu.VMEM((2, Q), f32),
             pltpu.VMEM((2, Q), f32),
             pltpu.VMEM((NX * NZ, 2, Q), f32),
             dma((7,)),
+            dma((4,)),
             dma((NCH,)),
             dma(()),
             dma((NCH,)),
@@ -399,6 +449,8 @@
             dma((2,)),
             dma((2,)),
             dma((4,)),
+            dma(()),
+            dma(()),
             dma(()),
             dma(()),
             dma(()),
@@ -417,6 +469,18 @@
             next_token,
         ))
     )
+    ensemble, nll = pl.pallas_call(
+        finish,
+        out_shape=(
+            jax.ShapeDtypeStruct((Q, NB * BLOCK), f32),
+            jax.ShapeDtypeStruct((1, Q), f32),
+        ),
+        in_specs=[vmem] * 6,
+        out_specs=(pl.BlockSpec(memory_space=pl.ANY),) * 2,
+        scratch_shapes=[pltpu.VMEM((Q, NB * BLOCK), f32), dma((NCH + 1,))],
+        compiler_params=pltpu.CompilerParams(vmem_limit_bytes=32 * 2**20),
+        name="finish",
+    )(*parts)
     return ensemble, nll.reshape(Q)
 
 

time: 46.1 us -> 44.3 us (0.961)
  local copies, waits for them, and re-layouts: 1.39 us -> 0 us
  Pallas kernels: 43.4 us -> 42.9 us
    unnamed x2 -> x0, local copies, waits for them, and re-layouts: 1.39 us -> none
    pallas_call x1 -> x2, Pallas kernels: 43.4 us -> 42.9 us  [the longest x1 41.8 us: on_device(): pl.pallas_call(kernel, out_shape=(pltpu.VMEM((NCH, Q, CW), f32), pltpu.VM...]
where the time goes in v3:
time: 44.3 us; the launch traced here: 44.1 us
  Pallas kernels  42.9 us (97%)
  between operations  1.29 us (3%)
    pallas_call x1, Pallas kernels, on_device(): pl.pallas_call(kernel, out_shape=(pltpu.VMEM((NCH, Q, CW), f32), pltpu.VM...  41.8 us
    pallas_call x1, Pallas kernels, on_device(): pl.pallas_call(finish, out_shape=(jax.ShapeDtypeStruct((Q, NB * BLOCK), f...  1.1 us

profile of v3, /device:TPU:1, one launch (start us, length us, event | category | flops | bytes accessed | tf_op | source)
XLA Modules:
  0.0 44.1 jit_solution(12003427348436396624)
XLA Ops:
  1.3 41.8 %ensemble.1 = (f32[6,128,256]{2,1,0:T(8,128)S(1)}, f32[3,128,512]{2,1,0:T(8,128)S(1)}, f32[6,1,128]{2,1,0:T(1,128)S(1)}, f32[1,128]{1,0:T(1,128)S(1)}, f32[1,128]{1,0:T(1,128)S(1)}, /*index=5*/f32[1,128]{1,0:T(1,128)S(1)}) custom-call(bf16[1,512,2048]{2,1,0:T(8,128)(2,1)} %hid.1, bf16[1,2048]{1,0:T(2,128)(2,1)} %gain.1, bf16[1,2048,1536]{2,1,0:T(8,128)(2,1)} %head.1, ...), custom_call_target="tpu_custom_call" | custom-call | flops 6442450944 | bytes 12582912 | tf_op jit(solution)/shard_map/ensemble/pallas_call | solution.py:397
  43.0 1.1 %finish.1 = (f32[128,1536]{1,0:T(8,128)}, f32[1,128]{1,0:T(1,128)}) custom-call(f32[6,128,256]{2,1,0:T(8,128)S(1)} %get-tuple-element.10.el, f32[3,128,512]{2,1,0:T(8,128)S(1)} %get-tuple-element.11.mp_buf, f32[6,1,128]{2,1,0:T(1,128)S(1)} %get-tuple-element.12.l_fac, f32[1,128]{1,0:T(1,128)S(1)} %get-tuple-element.13.m_fac, ...), custom_call_target="tpu_custom_call" | custom-call | tf_op jit(solution)/shard_map/finish/pallas_call | solution.py:472

commit v4 on v3

--- a/solution.py
+++ b/solution.py
@@ -111,9 +111,13 @@
         else:
             own_sq[...] = sq
 
-    def y_copy(j, k):
+    def halves(j):
+        return ((0, Q),) if j < NCH - 1 else ((0, 48), (48, 48), (96, 32))
+
+    def y_copy(j, k, h):
+        rows = pl.ds(*halves(j)[h])
         return pltpu.make_async_remote_copy(
-            src_ref=snd.at[j, k], dst_ref=rcv.at[j, k], send_sem=ys, recv_sem=yr.at[j],
+            src_ref=snd.at[j, k, rows], dst_ref=rcv.at[j, k, rows], send_sem=ys, recv_sem=yr.at[j + h],
             device_id=peers[k], device_id_type=MESH,
         )
 
@@ -140,9 +144,12 @@
 
     def send(j):
         for k in (2, 0, 1):
-            y_copy(j, k).start()
+            y_copy(j, k, 0).start()
         for k in range(3):
             ym_copy(j, k).start()
+        for h in range(1, len(halves(j))):
+            for k in (2, 0, 1):
+                y_copy(j, k, h).start()
 
     def wait_all(ref, sem):
         pltpu.make_async_copy(ref, ref, sem).wait()
@@ -175,23 +182,21 @@
 
     has = (v < 63, v > 0)
 
-    def halo(j, d):
+    def halo(buf, j, d, rows, send, recv):
         target, slot = (((m, v_up, r), j), ((m, v_down, r), 2 * NCH + j))[d]
-        return [
-            pltpu.make_async_remote_copy(
-                src_ref=buf.at[NCH + j], dst_ref=buf.at[slot], send_sem=send.at[d], recv_sem=recv.at[d],
-                device_id=target, device_id_type=MESH,
-            )
-            for buf, send, recv in ((pq, hs, hr), (pm, hms, hmr))
-        ]
-
-    def halo_start(j):
+        return pltpu.make_async_remote_copy(
+            src_ref=buf.at[NCH + j, rows], dst_ref=buf.at[slot, rows], send_sem=send.at[d], recv_sem=recv.at[d],
+            device_id=target, device_id_type=MESH,
+        )
+
+    def halo_start(j, h):
         for d in range(2):
 
             @pl.when(has[d])
             def _(d=d):
-                for cp in halo(j, d):
-                    cp.start()
+                halo(pq, j, d, pl.ds(*halves(j)[h]), hs, hr).start()
+                if h == len(halves(j)) - 1:
+                    halo(pm, j, d, pl.ds(0, 1), hms, hmr).start()
 
     for cp in lists:
         cp.wait()
@@ -205,7 +210,6 @@
 
     scale_own = scale_other = None
     for j in range(NCH):
-        wait_all(rcv.at[j], yr.at[j])
         if j != 1:
             wait_all(rcvm.at[j], ymr.at[j])
         if j == 0:
@@ -213,20 +217,29 @@
             sq = [rcvm[1, k, 1:2, :] for k in range(3)]
             scale_own = lax.rsqrt((own_sq[...] + sq[2]) * (1.0 / 4096.0) + 1e-05)
             scale_other = lax.rsqrt((sq[0] + sq[1]) * (1.0 / 4096.0) + 1e-05)
-        near, cross, far_term = (
-            rcv[j, k].astype(jnp.float32)
-            * to_col(rcvm[j, k, 0:1, :] * (scale_own if k == 2 else scale_other))
-            for k in range(3)
-        )
-        lg[m] = own[j] * to_col(scale_own) + far_term
-        lg[1 - m] = near + cross
-        logits = lg[1]
-        top = jnp.max(logits, axis=1, keepdims=True)
-        e = jnp.exp(logits - top)
-        pq[NCH + j] = e.astype(jnp.bfloat16)
-        pm[NCH + j] = to_row(top)
-        halo_start(j)
-        q_sums[j] = to_row(jnp.sum(e, axis=1, keepdims=True))
+        own_col = to_col(scale_own)
+        cols = [
+            to_col(rcvm[j, k, 0:1, :] * (scale_own if k == 2 else scale_other)) for k in range(3)
+        ]
+        q_tops, q_parts = [], []
+        for h, (first, count) in enumerate(halves(j)):
+            at = slice(first, first + count)
+            wait_all(rcv.at[j, :, pl.ds(first, count)], yr.at[j + h])
+            near, cross, far_term = (
+                rcv[j, k, at].astype(jnp.float32) * cols[k][at] for k in range(3)
+            )
+            lg[m, at] = own[j, at] * own_col[at] + far_term
+            lg[1 - m, at] = near + cross
+            logits = lg[1, at]
+            top = jnp.max(logits, axis=1, keepdims=True)
+            e = jnp.exp(logits - top)
+            pq[NCH + j, at] = e.astype(jnp.bfloat16)
+            q_tops.append(top)
+            q_parts.append(jnp.sum(e, axis=1, keepdims=True))
+            if h == len(halves(j)) - 1:
+                pm[NCH + j] = to_row(jnp.concatenate(q_tops, axis=0))
+            halo_start(j, h)
+        q_sums[j] = to_row(jnp.concatenate(q_parts, axis=0))
         logits = lg[0]
         top = jnp.max(logits, axis=1, keepdims=True)
         e = jnp.exp(logits - top)
@@ -430,8 +443,8 @@
             pltpu.VMEM((NCH, 1, Q), f32),
             pltpu.VMEM((NCH, 1, Q), f32),
             pltpu.VMEM((NCH, 1, Q), f32),
-            pltpu.VMEM((4, Q), f32),
-            pltpu.VMEM((4, Q), f32),
+            pltpu.VMEM((3, Q), f32),
+            pltpu.VMEM((3, Q), f32),
             pltpu.VMEM((NX * NZ, 2, Q), f32),
             pltpu.VMEM((NX * NZ, 1, Q), f32),
             pltpu.VMEM((2, Q), f32),
@@ -441,7 +454,7 @@
             dma((4,)),
             dma((NCH,)),
             dma(()),
-            dma((NCH,)),
+            dma((NCH + 2,)),
             dma(()),
             dma((NCH,)),
             dma((2,)),
@@ -477,7 +490,7 @@
         ),
         in_specs=[vmem] * 6,
         out_specs=(pl.BlockSpec(memory_space=pl.ANY),) * 2,
-        scratch_shapes=[pltpu.VMEM((Q, NB * BLOCK), f32), dma((NCH + 1,))],
+        scratch_shapes=[pltpu.VMEM((Q, NB * BLOCK), f32), dma((NCH + 2,))],
         compiler_params=pltpu.CompilerParams(vmem_limit_bytes=32 * 2**20),
         name="finish",
     )(*parts)

time: 44.3 us -> 43.5 us (0.982)
  Pallas kernels: 42.9 us -> 42.1 us
    pallas_call x1, Pallas kernels: 41.8 us -> 41 us  [on_device(): pl.pallas_call(kernel, out_shape=(pltpu.VMEM((NCH, Q, CW), f32), pltpu.VM...]
where the time goes in v4:
time: 43.5 us; the launch traced here: 43.3 us
  Pallas kernels  42.1 us (97%)
  between operations  1.29 us (3%)
    pallas_call x1, Pallas kernels, on_device(): pl.pallas_call(kernel, out_shape=(pltpu.VMEM((NCH, Q, CW), f32), pltpu.VM...  41 us
    pallas_call x1, Pallas kernels, on_device(): pl.pallas_call(finish, out_shape=(jax.ShapeDtypeStruct((Q, NB * BLOCK), f...  1.11 us

profile of v4, /device:TPU:1, one launch (start us, length us, event | category | flops | bytes accessed | tf_op | source)
XLA Modules:
  0.0 43.3 jit_solution(7270239410497159747)
XLA Ops:
  1.3 41.0 %ensemble.1 = (f32[6,128,256]{2,1,0:T(8,128)S(1)}, f32[3,128,512]{2,1,0:T(8,128)S(1)}, f32[6,1,128]{2,1,0:T(1,128)S(1)}, f32[1,128]{1,0:T(1,128)S(1)}, f32[1,128]{1,0:T(1,128)S(1)}, /*index=5*/f32[1,128]{1,0:T(1,128)S(1)}) custom-call(bf16[1,512,2048]{2,1,0:T(8,128)(2,1)} %hid.1, bf16[1,2048]{1,0:T(2,128)(2,1)} %gain.1, bf16[1,2048,1536]{2,1,0:T(8,128)(2,1)} %head.1, ...), custom_call_target="tpu_custom_call" | custom-call | flops 6442450944 | bytes 12582912 | tf_op jit(solution)/shard_map/ensemble/pallas_call | solution.py:410
  42.2 1.1 %finish.1 = (f32[128,1536]{1,0:T(8,128)}, f32[1,128]{1,0:T(1,128)}) custom-call(f32[6,128,256]{2,1,0:T(8,128)S(1)} %get-tuple-element.10.el, f32[3,128,512]{2,1,0:T(8,128)S(1)} %get-tuple-element.11.mp_buf, f32[6,1,128]{2,1,0:T(1,128)S(1)} %get-tuple-element.12.l_fac, f32[1,128]{1,0:T(1,128)S(1)} %get-tuple-element.13.m_fac, ...), custom_call_target="tpu_custom_call" | custom-call | tf_op jit(solution)/shard_map/finish/pallas_call | solution.py:485

commit v5 on v4

--- a/solution.py
+++ b/solution.py
@@ -319,10 +319,11 @@
     ]
     mass = jnp.zeros((Q, 1), jnp.float32)
     tok_m = jnp.zeros((Q, 1), jnp.float32)
+    terms = [
+        prods[2 * s] * factors[2 * s] + prods[2 * s + 1] * factors[2 * s + 1] for s in range(4)
+    ]
     for t in range(NB):
-        total = sum(
-            prods[s] * (factors[s] * (target[s] == t).astype(jnp.float32)) for s in range(8)
-        )
+        total = sum(terms[s] * (target[2 * s] == t).astype(jnp.float32) for s in range(4))
         mp_buf[t] = total
         mass = mass + jnp.sum(total, axis=1, keepdims=True)
         tok_m = tok_m + at_token(t * BLOCK, total)

time: 43.5 us -> 43.3 us (level)
  no operation moved by 1% of the time
where the time goes in v5:
time: 43.3 us; the launch traced here: 43.2 us
  Pallas kernels  41.9 us (97%)
  between operations  1.29 us (3%)
    pallas_call x1, Pallas kernels, on_device(): pl.pallas_call(kernel, out_shape=(pltpu.VMEM((NCH, Q, CW), f32), pltpu.VM...  40.8 us
    pallas_call x1, Pallas kernels, on_device(): pl.pallas_call(finish, out_shape=(jax.ShapeDtypeStruct((Q, NB * BLOCK), f...  1.11 us

profile of v5, /device:TPU:1, one launch (start us, length us, event | category | flops | bytes accessed | tf_op | source)
XLA Modules:
  0.0 43.2 jit_solution(6134189632674050323)
XLA Ops:
  1.3 40.8 %ensemble.1 = (f32[6,128,256]{2,1,0:T(8,128)S(1)}, f32[3,128,512]{2,1,0:T(8,128)S(1)}, f32[6,1,128]{2,1,0:T(1,128)S(1)}, f32[1,128]{1,0:T(1,128)S(1)}, f32[1,128]{1,0:T(1,128)S(1)}, /*index=5*/f32[1,128]{1,0:T(1,128)S(1)}) custom-call(bf16[1,512,2048]{2,1,0:T(8,128)(2,1)} %hid.1, bf16[1,2048]{1,0:T(2,128)(2,1)} %gain.1, bf16[1,2048,1536]{2,1,0:T(8,128)(2,1)} %head.1, ...), custom_call_target="tpu_custom_call" | custom-call | flops 6442450944 | bytes 12582912 | tf_op jit(solution)/shard_map/ensemble/pallas_call | solution.py:411
  42.1 1.1 %finish.1 = (f32[128,1536]{1,0:T(8,128)}, f32[1,128]{1,0:T(1,128)}) custom-call(f32[6,128,256]{2,1,0:T(8,128)S(1)} %get-tuple-element.10.el, f32[3,128,512]{2,1,0:T(8,128)S(1)} %get-tuple-element.11.mp_buf, f32[6,1,128]{2,1,0:T(1,128)S(1)} %get-tuple-element.12.l_fac, f32[1,128]{1,0:T(1,128)S(1)} %get-tuple-element.13.m_fac, ...), custom_call_target="tpu_custom_call" | custom-call | tf_op jit(solution)/shard_map/finish/pallas_call | solution.py:486
